TPU v7x, 32 devices: a whole 2x2x4 slice. The times are simulated.
32 devices in a mesh: wide: 8 (over z, x), narrow: 4 (over y, core).
Axes of the slice: x: 2, y: 2, z: 4, core: 2. Of those that a mesh axis runs over, the one named last changes fastest.
Arguments:
- sigma_irr: float32 [224, 2, 2, 1600], P('wide'), may hold values from -6 to 6
- star_irr: int32 [8, 8, 32], P('wide', 'narrow'), may hold values from 0 to 223, as said below
- star_sym: int32 [8, 8, 32], P('wide', 'narrow'), may hold values from 0 to 47
- rep_matrices: float32 [48, 40, 40], replicated, may hold values from -1 to 1
Outputs:
- sigma_lattice: float32 [8, 8, 32, 2, 2, 1600], P('narrow', None, 'wide')
Inputs may be any that keep to these rules, and one draw needn't show every extreme that they name: Among the 1 x 2 x 32 mesh points of one device, at most 16 have an irreducible point held by one owner (star_irr // 28); on every device some owner is named exactly 16 times.
All inputs are finite; a program needn't handle non-finite values.
Results may differ from a plain program's by a relative error of at most 0.00007.
Values sent between devices are 32-bit elements; how exact they have to be, the bound alone decides.
A program may use at most 64 MiB of HBM per device.

v0:
```python
import math

import jax
import jax.numpy as jnp
from jax import lax
from jax.sharding import PartitionSpec as P


def transform(values, position):
    length = values.shape[position]
    ramp_index = jnp.arange(length, dtype=jnp.int32)
    angles = (
        2.0
        * math.pi
        / length
        * (ramp_index[:, None] * ramp_index[None, :] % length).astype(jnp.float32)
    )
    factor = 1.0 / math.sqrt(length)
    cosine_table = jnp.cos(angles) * factor
    sine_table = jnp.sin(angles) * factor
    real_part = values[:, :, :, :, 0]
    imag_part = values[:, :, :, :, 1]

    def apply_table(matrix, operand):
        product = jnp.tensordot(
            matrix, operand, axes=([1], [position]), precision=lax.Precision.HIGHEST
        )
        return jnp.moveaxis(product, 0, position)

    new_real = apply_table(cosine_table, real_part) + apply_table(sine_table, imag_part)
    new_imag = apply_table(cosine_table, imag_part) - apply_table(sine_table, real_part)
    return jnp.stack([new_real, new_imag], axis=4)


def finish(returned, position, rotation, shape_out):
    orbitals = rotation.shape[1]
    flattened = returned.reshape((-1,) + returned.shape[2:])
    gathered = flattened[position]
    square = gathered.reshape(gathered.shape[:3] + (orbitals, orbitals))
    partial_product = jnp.einsum(
        "kab,kfcbd->kfcad", rotation, square, precision=lax.Precision.HIGHEST
    )
    turned = jnp.einsum(
        "kfcad,ked->kfcae", partial_product, rotation, precision=lax.Precision.HIGHEST
    )
    values = turned.reshape(shape_out + gathered.shape[1:])
    values = transform(values, 2)
    values = lax.all_to_all(values, "wide", split_axis=2, concat_axis=0, tiled=True)
    values = transform(values, 0)
    values = lax.all_to_all(values, "narrow", split_axis=0, concat_axis=1, tiled=True)
    return transform(values, 1)


def local(sigma_irr, star_irr, star_sym, rep_matrices):
    wide_count = lax.axis_size("wide")
    held_rows = sigma_irr.shape[0]
    points = star_irr.size
    capacity = 2 * points // wide_count
    flat_irr = star_irr.reshape(-1)
    owners = flat_irr // held_rows
    local_rows = flat_irr - owners * held_rows
    member = (owners[:, None] == jnp.arange(wide_count, dtype=jnp.int32)[None, :]).astype(jnp.int32)
    before = jnp.cumsum(member, axis=0) - member
    slot_of = jnp.sum(before * member, axis=1)
    position = owners * capacity + slot_of
    requests = jnp.zeros((wide_count * capacity,), jnp.int32).at[position].set(local_rows)
    requests = requests.reshape(wide_count, capacity)
    asked = lax.all_to_all(requests, "wide", split_axis=0, concat_axis=0, tiled=True)
    rotation = rep_matrices[star_sym.reshape(-1)]
    shape_out = star_irr.shape
    chosen = sigma_irr[asked]
    returned = lax.all_to_all(chosen, "wide", split_axis=0, concat_axis=0, tiled=True)
    return finish(returned, position, rotation, shape_out)


def solution(mesh):
    placed = (
        P("wide", None, None, None),
        P("wide", "narrow", None),
        P("wide", "narrow", None),
        P(),
    )
    return jax.shard_map(
        local,
        mesh=mesh,
        in_specs=placed,
        out_specs=P("narrow", None, "wide", None, None, None),
        check_vma=False,
    )
```

profile of v0, /device:TPU:11, one launch (start us, length us, event | category | flops | bytes accessed | tf_op | source)
XLA Modules:
  0.0 225.6 jit_solution(5844481214250978227)
XLA Ops:
  3.6 8.7 %all_to_all.53 = s32[8,1,16]{2,1,0:T(1,128)S(1)} all-to-all(s32[8,1,16]{2,1,0:T(1,128)S(1)} %bitcast.137), channel_id=1, replica_groups=mesh['wide'=8,'narrow'=4] {'wide'}, dimensions={0} | all-to-all | bytes 1024 | tf_op jit(solution)/shard_map/all_to_all | solution.py:68
  12.4 5.8 %gather_fusion = f32[128,2,2,1600]{3,2,1,0:T(2,128)} fusion(f32[28,2,2,1600]{3,2,1,0:T(2,128)S(1)} %copy-done, s32[1024]{0:T(1024)S(1)} %pad_clamp_fusion.2), kind=kCustom, calls=%fused_computation | custom fusion | bytes 6554112 | tf_op jit(solution)/shard_map/gather | solution.py:71
  18.2 6.6 %all-to-all-start.1 = ((f32[8,16,2,2,1600]{4,3,2,1,0:T(2,128)}), f32[8,16,2,2,1600]{4,3,2,1,0:T(2,128)}, u32[]{:S(2)}, u32[]{:S(2)}) async-start(f32[8,16,2,2,1600]{4,3,2,1,0:T(2,128)} %bitcast.132), calls=%async_computation.1 | async-start | bytes 6815744 | tf_op jit(solution)/shard_map/all_to_all | solution.py:72
  26.0 72.6 %all-to-all-done.1 = f32[8,16,2,2,1600]{4,3,2,1,0:T(2,128)} async-done(((f32[8,16,2,2,1600]{4,3,2,1,0:T(2,128)}), f32[8,16,2,2,1600]{4,3,2,1,0:T(2,128)}, u32[]{:S(2)}, u32[]{:S(2)}) %all-to-all-start.1) | async-done | bytes 3276832 | tf_op jit(solution)/shard_map/all_to_all | solution.py:72
  98.6 5.4 %gather_fusion.1 = f32[64,2,2,1600]{3,2,1,0:T(2,128)} fusion(f32[128,2,2,1600]{3,2,1,0:T(2,128)} %bitcast.10, s32[1024]{0:T(1024)S(1)} %pad_clamp_fusion.1), kind=kCustom, calls=%fused_computation.1 | custom fusion | bytes 3277056 | tf_op jit(solution)/shard_map/gather | solution.py:38
  104.0 4.5 %copy.41 = f32[64,2,2,1600]{0,3,2,1:T(8,128)} copy(f32[64,2,2,1600]{3,2,1,0:T(2,128)} %gather_fusion.1) | data formatting | bytes 3276800 | tf_op jit(solution)/shard_map/gather | solution.py:38
  108.5 5.5 %copy.43 = f32[64,2,2,40,40]{3,4,2,1,0:T(8,128)} copy(f32[64,2,2,40,40]{0,4,3,2,1:T(8,128)} %bitcast.133) | data formatting | bytes 3276800 | tf_op jit(solution)/shard_map/reshape | solution.py:39
  114.0 6.9 %convolution_bitcast_fusion = f32[64,2,2,40,40]{3,4,2,1,0:T(8,128)S(1)} fusion(f32[64,2,2,40,40]{3,4,2,1,0:T(8,128)} %copy.43, f32[64,40,40]{2,1,0:T(8,128)S(1)} %gather_fusion.2), kind=kOutput, calls=%fused_computation.18 | convolution fusion | flops 196608000 | bytes 3686400 | tf_op jit(solution)/shard_map/kab,kfcbd->kfcad/dot_general | solution.py:40
  120.9 10.3 %fusion = f32[64,2,2,40,40]{4,3,0,2,1:T(8,128)} fusion(f32[64,2,2,40,40]{3,4,2,1,0:T(8,128)S(1)} %convolution_bitcast_fusion, f32[64,40,40]{2,1,0:T(8,128)S(1)} %gather_fusion.2), kind=kOutput, calls=%fused_computation.4 | convolution fusion | flops 196608000 | bytes 3686400 | tf_op jit(solution)/shard_map/kfcad,ked->kfcae/dot_general | solution.py:43
  131.1 4.2 %reshape.176 = f32[1,2,32,2,2,1600]{5,2,1,4,3,0:T(8,128)S(1)} reshape(f32[64,2,2,40,40]{4,3,0,2,1:T(8,128)} %fusion) | data formatting | bytes 3276800 | tf_op jit(solution)/shard_map/reshape | solution.py:46
  135.5 0.9 fusion.10
  136.4 0.9 fusion.11
  137.4 0.9 fusion.2
  138.3 0.9 fusion.3
  139.4 1.3 copy.48
  140.7 43.6 %all_to_all.54 = f32[1,2,32,2,2,1600]{5,3,1,4,0,2:T(2,128)S(1)} all-to-all(f32[1,2,32,2,2,1600]{5,3,1,4,0,2:T(2,128)S(1)} %copy.48), channel_id=1, replica_groups=mesh['wide'=8,'narrow'=4] {'wide'}, dimensions={2} | all-to-all | bytes 3276800 | tf_op jit(solution)/shard_map/all_to_all | solution.py:48
  184.3 1.0 copy.77
  187.1 0.9 fusion.5
  189.9 24.9 %all_to_all.55 = f32[8,2,4,2,2,1600]{5,3,2,1,4,0:T(2,128)S(1)} all-to-all(f32[8,2,4,2,2,1600]{5,3,2,1,4,0:T(2,128)S(1)} %copy.51), channel_id=1, replica_groups=mesh['wide'=8,'narrow'=4] {'narrow'}, dimensions={0} | all-to-all | bytes 3276800 | tf_op jit(solution)/shard_map/all_to_all | solution.py:50
  214.8 2.1 copy.78
  216.9 2.5 %all_to_all.48 = f32[2,8,4,2,2,1600]{5,1,3,2,0,4:T(8,128)S(1)} reshape(f32[2,4,2,4,2,2,1600]{6,2,1,4,3,0,5:T(2,128)} %bitcast.136) | data formatting | bytes 3276800 | tf_op jit(solution)/shard_map/all_to_all | solution.py:50
  221.1 0.9 fusion.7
  222.0 0.9 fusion.6
  223.1 2.5 %copy.53 = f32[2,8,4,2,2,1600]{5,4,3,2,1,0:T(2,128)} copy(f32[2,8,4,2,2,1600]{5,1,3,2,0,4:T(8,128)S(1)} %pad_maximum_fusion.2) | data formatting | bytes 3276800 | tf_op jit(solution)/shard_map/stack | solution.py:32
  (37 shorter events, 10.6 us)
Async XLA Ops:
  0.0 12.4 %copy-start = (f32[28,2,2,1600]{3,2,1,0:T(2,128)S(1)}, f32[28,2,2,1600]{3,2,1,0:T(2,128)}, u32[]{:S(2)}) copy-start(f32[28,2,2,1600]{3,2,1,0:T(2,128)} %param.4) | copy-start | bytes 2150404
  18.2 6.6 %copy-start.2 = (s32[1,2,32]{2,1,0:T(2,128)S(1)}, s32[1,2,32]{2,1,0:T(2,128)}, u32[]{:S(2)}) copy-start(s32[1,2,32]{2,1,0:T(2,128)} %param.6) | copy-start | bytes 772
  18.2 6.7 %copy-start.1 = (f32[48,40,40]{0,2,1:T(8,128)S(1)}, f32[48,40,40]{0,2,1:T(8,128)}, u32[]{:S(2)}) copy-start(f32[48,40,40]{0,2,1:T(8,128)} %param.7) | copy-start | bytes 921604
  18.2 80.3 %all-to-all-start.1 = ((f32[8,16,2,2,1600]{4,3,2,1,0:T(2,128)}), f32[8,16,2,2,1600]{4,3,2,1,0:T(2,128)}, u32[]{:S(2)}, u32[]{:S(2)}) async-start(f32[8,16,2,2,1600]{4,3,2,1,0:T(2,128)} %bitcast.132), calls=%async_computation.1 | async-start | bytes 6815744 | tf_op jit(solution)/shard_map/all_to_all | solution.py:72
where the time goes:
time: 230 us; the launch traced here: 226 us
  blocking collectives  77.2 us (34%)
  waiting for transfers between devices  72.6 us (32%)
  local copies, waits for them, and re-layouts  38.8 us (17%)
  matrix products  28 us (12%)
  starting transfers between devices  6.56 us (3%)
    all_to_all x1, waiting for transfers between devices, local(): lax.all_to_all(chosen, 'wide', split_axis=0, concat_axis=0, tiled=True)  72.6 us
    all_to_all x1, blocking collectives, finish(): lax.all_to_all(values, 'wide', split_axis=2, concat_axis=0, tiled=True)  43.6 us
    all_to_all x1, blocking collectives, finish(): lax.all_to_all(values, 'narrow', split_axis=0, concat_axis=1, tiled=True)  24.9 us
    dot_general x12, matrix products, apply_table(): jnp.tensordot(matrix, operand, axes=([1], [position]), precision=lax.Prec...  10.9 us
    dot_general x1, matrix products, finish(): jnp.einsum('kfcad,ked->kfcae', partial_product, rotation, precision=lax.P...  10.3 us
    gather x2, local copies, waits for them, and re-layouts, finish(): gathered = flattened[position]  9.94 us
    all_to_all x1, blocking collectives, local(): lax.all_to_all(requests, 'wide', split_axis=0, concat_axis=0, tiled=True)  8.7 us
    dot_general x1, matrix products, finish(): jnp.einsum('kab,kfcbd->kfcad', rotation, square, precision=lax.Precision....  6.86 us
  transfers between devices with their start and end apart: 1, of which 1 were waited for; matrix products, arithmetic and copies ran while one was open for 1% of the time, Pallas kernels for 0%

commit v1 on v0

v1 whole, which is shorter than its diff:
```python
import functools
import math

import jax
import jax.numpy as jnp
from jax import lax
from jax.experimental import pallas as pl
from jax.experimental.pallas import tpu as pltpu
from jax.sharding import PartitionSpec as P

MESH = pl.DeviceIdType.MESH
LANES = 128
SUB = 8


def twiddle(value, step, length):
    real, imag = value
    step %= length
    if step == 0:
        return value
    if 4 * step == length:
        return imag, -real
    if 2 * step == length:
        return -real, -imag
    if 8 * step == length:
        root = math.sqrt(0.5)
        return (real + imag) * root, (imag - real) * root
    if 8 * step == 3 * length:
        root = math.sqrt(0.5)
        return (imag - real) * root, -(real + imag) * root
    cosine = math.cos(2 * math.pi * step / length)
    sine = math.sin(2 * math.pi * step / length)
    return real * cosine + imag * sine, imag * cosine - real * sine


def fourier(values):
    length = len(values)
    if length == 1:
        return values
    even = fourier(values[0::2])
    odd = fourier(values[1::2])
    half = length // 2
    odd = [twiddle(odd[i], i, length) for i in range(half)]
    low = [(a[0] + b[0], a[1] + b[1]) for a, b in zip(even, odd)]
    high = [(a[0] - b[0], a[1] - b[1]) for a, b in zip(even, odd)]
    return low + high


def pack(blocks, width):
    total = width * len(blocks)
    tiles = -(-total // LANES)
    lane = lax.broadcasted_iota(jnp.int32, blocks[0].shape, 1)
    made = [None] * tiles
    for index, block in enumerate(blocks):
        tile, offset = divmod(index * width, LANES)
        moved = pltpu.roll(block, offset, 1) if offset else block
        made[tile] = moved if made[tile] is None else jnp.where(lane < offset, made[tile], moved)
        if offset + width > LANES:
            made[tile + 1] = moved
    return made


def unpack(tiles, index, width):
    tile, offset = divmod(index * width, LANES)
    block = tiles[tile]
    if offset + width > LANES:
        lane = lax.broadcasted_iota(jnp.int32, block.shape, 1)
        block = jnp.where(lane >= offset, block, tiles[tile + 1])
    return pltpu.roll(block, LANES - offset, 1) if offset else block


def halves(value):
    high = value.astype(jnp.bfloat16)
    low = (value - high.astype(jnp.float32)).astype(jnp.bfloat16)
    return high, low


def unfold_kernel(
    held, per_tile, orbitals, scale, irr_ref, sym_ref, blocks_ref, right_ref, left_ref, out_ref, unfolded
):
    wide, steps, _, rows_y, _, _ = out_ref.shape
    points = irr_ref.shape[0]
    length = points // rows_y
    lane = lax.broadcasted_iota(jnp.int32, (orbitals, LANES), 1)
    first = lane < orbitals

    def one_point(k, carry):
        irr = irr_ref[k]
        sym = sym_ref[k]
        owner = irr // held
        row = irr - owner * held
        tile = row // per_tile
        shift = (row - tile * per_tile) * orbitals
        block = blocks_ref[owner, :, pl.ds(pl.multiple_of(tile * LANES, LANES), LANES)]
        start = pl.multiple_of((per_tile - 1) * orbitals - shift, SUB)
        weights = right_ref[sym, pl.ds(start, LANES), :]
        high, low = halves(weights)
        block_high, block_low = halves(block)
        product = jnp.dot(
            jnp.concatenate([block_high, block_low], axis=1),
            jnp.concatenate(
                [
                    jnp.concatenate([high, low], axis=1),
                    jnp.concatenate([high, jnp.zeros_like(low)], axis=1),
                ],
                axis=0,
            ),
            preferred_element_type=jnp.float32,
        )
        product = product[:, :LANES] + product[:, LANES:]
        parts = []
        for c in range(2):
            base = 2 * c * orbitals
            parts.append(
                jnp.where(first, product[base : base + orbitals], product[base + orbitals : base + 2 * orbitals])
            )
        half = jnp.concatenate(parts, axis=1)
        half_high = half.astype(jnp.bfloat16).astype(jnp.float32)
        stacked = jnp.concatenate(
            [half_high, half - half_high, half_high, jnp.zeros((LANES - 3 * orbitals, 2 * LANES), jnp.float32)],
            axis=0,
        )
        turned = jnp.dot(
            left_ref[sym].astype(jnp.bfloat16),
            stacked.astype(jnp.bfloat16),
            preferred_element_type=jnp.float32,
        )
        unfolded[0, k] = turned[:, :LANES]
        unfolded[1, k] = turned[:, LANES:]
        return carry

    lax.fori_loop(0, points, one_point, 0, unroll=4)

    per_dest = length // wide

    def one_transform(at, carry):
        y = at // steps
        step = at - y * steps
        rows = pl.ds(pl.multiple_of(step * SUB, SUB), SUB)
        values = [(unfolded[0, y * length + z, rows, :], unfolded[1, y * length + z, rows, :]) for z in range(length)]
        result = fourier(values)
        for dest in range(wide):
            for c in range(2):
                made = pack([result[dest * per_dest + i][c] * scale for i in range(per_dest)], 2 * orbitals)
                for j, tile in enumerate(made):
                    out_ref[dest, step, c, y, j * SUB : (j + 1) * SUB, :] = tile
        return carry

    lax.fori_loop(0, rows_y * steps, one_transform, 0)


def exchange_kernel(
    orbitals, y_ref, out_ref, from_wide, to_narrow, from_narrow, send_wide, recv_wide, send_narrow, recv_narrow, own
):
    wide, steps, _, rows_y, tile_rows, _ = y_ref.shape
    narrow, _, rows_x = to_narrow.shape[:3]
    tiles = tile_rows // SUB
    me_wide = lax.axis_index("wide")
    me_narrow = lax.axis_index("narrow")

    barrier = pltpu.get_barrier_semaphore()
    for i in range(1, wide):
        pl.semaphore_signal(barrier, inc=1, device_id=(lax.rem(me_wide + i, wide), me_narrow), device_id_type=MESH)
    for i in range(1, narrow):
        pl.semaphore_signal(barrier, inc=1, device_id=(me_wide, lax.rem(me_narrow + i, narrow)), device_id_type=MESH)
    pl.semaphore_wait(barrier, wide + narrow - 2)

    def wide_copy(step, i):
        peer = lax.rem(me_wide + i, wide)
        return pltpu.make_async_remote_copy(
            src_ref=y_ref.at[peer, step],
            dst_ref=from_wide.at[me_wide, step],
            send_sem=send_wide.at[step, i],
            recv_sem=recv_wide.at[step, i],
            device_id=(peer, me_narrow),
            device_id_type=MESH,
        )

    def narrow_copy(step, i):
        peer = lax.rem(me_narrow + i, narrow)
        return pltpu.make_async_remote_copy(
            src_ref=to_narrow.at[peer, step],
            dst_ref=from_narrow.at[me_narrow, step],
            send_sem=send_narrow.at[step, i],
            recv_sem=recv_narrow.at[step, i],
            device_id=(me_wide, peer),
            device_id_type=MESH,
        )

    for step in range(steps):
        for i in range(1, wide):
            wide_copy(step, i).start()
    own_copy = pltpu.make_async_copy(y_ref.at[me_wide], from_wide.at[me_wide], own.at[steps])
    own_copy.start()
    own_copy.wait()

    def finish(step):
        for i in range(1, narrow):
            narrow_copy(step, i).wait_recv()
        rows = slice(step * SUB, (step + 1) * SUB)

        def one(x, carry):
            made = []
            for j in range(tiles):
                at = slice(j * SUB, (j + 1) * SUB)
                made.append(
                    fourier(
                        [
                            (from_narrow[n, step, x, 0, y, at, :], from_narrow[n, step, x, 1, y, at, :])
                            for n in range(narrow)
                            for y in range(rows_y)
                        ]
                    )
                )
            for y in range(narrow * rows_y):
                for c in range(2):
                    line = [made[j][y][c] for j in range(tiles)]
                    for z in range(out_ref.shape[2]):
                        for f in range(2):
                            block = unpack(line, 2 * z + f, orbitals)
                            out_ref[x, y, z, f, c, rows, :] = block[:, :orbitals]
            return carry

        lax.fori_loop(0, rows_x, one, 0)

    for step in range(steps):
        for i in range(1, wide):
            wide_copy(step, i).wait_recv()

        def one(at, carry):
            y = at // tiles
            rows = pl.ds(pl.multiple_of((at - y * tiles) * SUB, SUB), SUB)
            values = [
                (from_wide[w, step, 0, y, rows, :], from_wide[w, step, 1, y, rows, :]) for w in range(wide)
            ]
            for x, pair in enumerate(fourier(values)):
                for c in range(2):
                    to_narrow[x // rows_x, step, x % rows_x, c, y, rows, :] = pair[c]
            return carry

        lax.fori_loop(0, rows_y * tiles, one, 0)
        for i in range(1, narrow):
            narrow_copy(step, i).start()
        mine = pltpu.make_async_copy(to_narrow.at[me_narrow, step], from_narrow.at[me_narrow, step], own.at[step])
        mine.start()
        mine.wait()
        if step:
            finish(step - 1)
    finish(steps - 1)
    for step in range(steps):
        for i in range(1, wide):
            wide_copy(step, i).wait_send()
        for i in range(1, narrow):
            narrow_copy(step, i).wait_send()


def spread_blocks(sigma_irr, orbitals, per_tile):
    held, freqs, parts, _ = sigma_irr.shape
    narrow = lax.axis_size("narrow")
    tiles = -(-held // per_tile)
    share = narrow // (freqs * parts)
    if share and orbitals // share % SUB == 0:
        axes = ("wide", "narrow")
        index = lax.axis_index("narrow")
        which, piece = index // share, index % share
        part, freq = which // freqs, which % freqs
        width = orbitals * orbitals // share
        own = lax.dynamic_slice(sigma_irr, (0, freq, part, piece * width), (held, 1, 1, width))
    else:
        axes = "wide"
        own = jnp.swapaxes(sigma_irr, 1, 2)
    own = own.reshape(held, -1, orbitals).transpose(1, 0, 2)
    rows = own.shape[0]
    own = jnp.pad(own, ((0, 0), (0, tiles * per_tile - held), (0, 0)))
    own = own.reshape(rows, tiles, per_tile * orbitals)
    own = jnp.pad(own, ((0, 0), (0, 0), (0, LANES - per_tile * orbitals)))
    own = own.reshape(rows, tiles * LANES)
    every = lax.all_gather(own, axes, axis=0, tiled=True)
    return every.reshape(lax.axis_size("wide"), freqs * parts * orbitals, tiles * LANES)


def local(sigma_irr, star_irr, star_sym, rep_matrices):
    wide, narrow = lax.axis_size("wide"), lax.axis_size("narrow")
    held, freqs, parts, _ = sigma_irr.shape
    orbitals = rep_matrices.shape[1]
    rows_y, length = star_irr.shape[1:]
    per_tile = LANES // orbitals
    per_dest = length // wide
    steps = orbitals // SUB
    tile_rows = SUB * -(-per_dest * freqs * orbitals // LANES)
    size_x, size_y = wide * star_irr.shape[0], narrow * rows_y
    rows_x = size_x // narrow

    blocks = spread_blocks(sigma_irr, orbitals, per_tile)
    turned = jnp.swapaxes(rep_matrices, 1, 2)
    before = (per_tile - 1) * orbitals
    right = jnp.pad(
        jnp.concatenate([turned, turned], axis=2),
        ((0, 0), (before, LANES - orbitals), (0, LANES - 2 * orbitals)),
    )
    high = lax.reduce_precision(rep_matrices, 8, 7)
    left = jnp.pad(
        jnp.concatenate([high, high, rep_matrices - high], axis=2), ((0, 0), (0, 0), (0, LANES - 3 * orbitals))
    )

    vmem = pl.BlockSpec(memory_space=pltpu.VMEM)
    smem = pl.BlockSpec(memory_space=pltpu.SMEM)
    sent = pl.pallas_call(
        functools.partial(
            unfold_kernel, held, per_tile, orbitals, 1.0 / math.sqrt(size_x * size_y * length)
        ),
        out_shape=jax.ShapeDtypeStruct((wide, steps, 2, rows_y, tile_rows, LANES), jnp.float32),
        in_specs=[smem, smem, vmem, vmem, vmem],
        out_specs=vmem,
        scratch_shapes=[pltpu.VMEM((2, rows_y * length, orbitals, LANES), jnp.float32)],
        compiler_params=pltpu.CompilerParams(vmem_limit_bytes=56 * 1024 * 1024),
    )(star_irr.reshape(-1), star_sym.reshape(-1), blocks, right, left)

    slots = (steps, 2, rows_y, tile_rows, LANES)
    middle = (narrow, steps, rows_x, 2, rows_y, tile_rows, LANES)
    result = pl.pallas_call(
        functools.partial(exchange_kernel, orbitals),
        out_shape=jax.ShapeDtypeStruct((rows_x, size_y, per_dest, freqs, 2, orbitals, orbitals), jnp.float32),
        in_specs=[vmem],
        out_specs=vmem,
        scratch_shapes=[
            pltpu.VMEM((wide,) + slots, jnp.float32),
            pltpu.VMEM(middle, jnp.float32),
            pltpu.VMEM(middle, jnp.float32),
            pltpu.SemaphoreType.DMA((steps, wide)),
            pltpu.SemaphoreType.DMA((steps, wide)),
            pltpu.SemaphoreType.DMA((steps, narrow)),
            pltpu.SemaphoreType.DMA((steps, narrow)),
            pltpu.SemaphoreType.DMA((steps + 1,)),
        ],
        compiler_params=pltpu.CompilerParams(
            collective_id=0, has_side_effects=True, vmem_limit_bytes=56 * 1024 * 1024
        ),
    )(sent)
    return result.reshape(result.shape[:5] + (orbitals * orbitals,))


def solution(mesh):
    placed = (
        P("wide", None, None, None),
        P("wide", "narrow", None),
        P("wide", "narrow", None),
        P(),
    )
    return jax.shard_map(
        local,
        mesh=mesh,
        in_specs=placed,
        out_specs=P("narrow", None, "wide", None, None, None),
        check_vma=False,
    )
```

time: 230 us -> 171 us (0.74); the launches traced: 226 us -> 171 us
  blocking collectives: 77.2 us -> 0 us
  Pallas kernels: 0 us -> 75.9 us
  matrix products: 28 us -> 0 us
  local copies, waits for them, and re-layouts: 38.8 us -> 13.8 us
  between operations: 0.24 us -> 13.5 us
  waiting for transfers between devices: 72.6 us -> 61.4 us
  starting transfers between devices: 6.56 us -> 0.01 us
  other arithmetic: 2.21 us -> 6.6 us
    all_to_all x3 -> x0, blocking collectives: 77.2 us -> none  [the longest x1 43.6 us: finish(): lax.all_to_all(values, 'wide', split_axis=2, concat_axis=0, tiled=True)]
    pallas_call x0 -> x2, Pallas kernels: none -> 75.9 us  [the longest x1 56.2 us: local(): pl.pallas_call(functools.partial(exchange_kernel, orbitals), out_shape=ja...]
    all_to_all x1 -> x0, waiting for transfers between devices: 72.6 us -> none  [local(): lax.all_to_all(chosen, 'wide', split_axis=0, concat_axis=0, tiled=True)]
    all_gather x0 -> x1, waiting for transfers between devices: none -> 61.4 us  [spread_blocks(): every = lax.all_gather(own, axes, axis=0, tiled=True)]
    dot_general x14 -> x0, matrix products: 28 us -> none  [the longest x12 10.9 us: apply_table(): jnp.tensordot(matrix, operand, axes=([1], [position]), precision=lax.Prec...]
    gather x4 -> x0, local copies, waits for them, and re-layouts: 16.4 us -> none  [the longest x2 9.94 us: finish(): gathered = flattened[position]]
    all_to_all x1 -> x0, starting transfers between devices: 6.56 us -> none  [local(): lax.all_to_all(chosen, 'wide', split_axis=0, concat_axis=0, tiled=True)]
    all_to_all x4 -> x0, local copies, waits for them, and re-layouts: 5.58 us -> none  [the longest x2 4.51 us: finish(): lax.all_to_all(values, 'narrow', split_axis=0, concat_axis=1, tiled=True)]
  transfers between devices with their start and end apart: 1 -> 1, of which waited for: 1 -> 1; matrix products, arithmetic and copies ran while one was open for 1% -> 7% of each run, Pallas kernels for 0% -> 0%
where the time goes in v1:
time: 171 us
  Pallas kernels  75.9 us (44%)
  waiting for transfers between devices  61.4 us (36%)
  local copies, waits for them, and re-layouts  13.8 us (8%)
  between operations  13.5 us (8%)
  other arithmetic  6.6 us (4%)
    all_gather x1, waiting for transfers between devices, spread_blocks(): every = lax.all_gather(own, axes, axis=0, tiled=True)  61.4 us
    pallas_call x1, Pallas kernels, local(): pl.pallas_call(functools.partial(exchange_kernel, orbitals), out_shape=ja...  56.2 us
    pallas_call x1, Pallas kernels, local(): pl.pallas_call(functools.partial(unfold_kernel, held, per_tile, orbitals,...  19.7 us
    reshape x1, local copies, waits for them, and re-layouts, local(): return result.reshape(result.shape[:5] + (orbitals * orbitals,))  6.22 us
    unnamed x12, local copies, waits for them, and re-layouts  3.7 us
  transfers between devices with their start and end apart: 1, of which 1 were waited for; matrix products, arithmetic and copies ran while one was open for 7% of the time, Pallas kernels for 0%

profile of v1, /device:TPU:11, one launch (start us, length us, event | category | flops | bytes accessed | tf_op | source)
XLA Modules:
  0.0 171.1 jit_solution(6659475316082019581)
XLA Ops:
  6.5 1.1 copy-done
  7.7 0.5 dynamic-slice_reduce_fusion
  8.2 0.3 reshape.23
  8.5 0.0 copy-start.2
  8.5 0.0 copy-start.3
  8.5 0.1 copy.18
  8.6 0.1 pad.16.clone
  8.7 0.2 reshape.24
  8.9 0.7 copy.21
  9.6 0.0 all-gather.2.cloned.1.call-update
  9.7 1.0 reduce_precision.3
  10.6 0.4 copy.13
  11.1 1.3 copy.14
  12.4 0.7 reshape.21.irr_ref
  13.0 0.0 copy-done.3
  13.0 0.7 reshape.22.sym_ref
  13.7 1.5 copy.16
  15.2 1.4 sub.9
  16.6 1.6 select_maximum_fusion.1.left_ref
  18.2 2.6 %select_maximum_fusion.right_ref = f32[48,208,128]{2,1,0:T(8,128)} fusion(f32[48,40,40]{2,1,0:T(8,128)S(1)} %bitcast.10), kind=kLoop, calls=%fused_computation.2 | loop fusion | flops 12779520 | bytes 5419008 | tf_op jit(solution)/shard_map/concatenate | solution.py:298
  20.8 61.4 %all-gather.2.cloned.1.call-done = f32[1280,1280]{1,0:T(8,128)} async-done(((f32[40,1280]{1,0:T(8,128)}), f32[1280,1280]{1,0:T(8,128)}) %all-gather.2.cloned.1.call-update) | async-done | bytes 6553616 | tf_op jit(solution)/shard_map/all_gather | solution.py:278
  82.2 19.7 %shard_map.46.y_ref = f32[8,5,2,2,24,128]{5,4,3,2,1,0:T(8,128)} custom-call(s32[64]{0:T(128)} %reshape.21.irr_ref, s32[64]{0:T(128)} %reshape.22.sym_ref, f32[8,160,1280]{2,1,0:T(8,128)} %bitcast.9, f32[48,208,128]{2,1,0:T(8,128)} %select_maximum_fusion.right_ref, f32[48,40,128]{2,1,0:T(8,128)} %select_maximum_fusion.1.left_ref), custom_call_target="tpu_custom_call" | custom-call | tf_op jit(solution)/shard_map/pallas_call | solution.py:308
  101.9 56.2 %shard_map.47 = f32[2,8,4,2,2,40,40]{6,5,4,3,2,1,0:T(8,128)} custom-call(f32[8,5,2,2,24,128]{5,4,3,2,1,0:T(8,128)} %shard_map.46.y_ref), custom_call_target="tpu_custom_call" | custom-call | tf_op jit(solution)/shard_map/pallas_call | solution.py:321
  158.1 6.2 %reshape.27 = f32[2,8,4,2,2,1600]{5,4,3,2,1,0:T(2,128)} reshape(f32[2,8,4,2,2,40,40]{6,5,4,3,2,1,0:T(8,128)} %shard_map.47) | data formatting | bytes 3276800 | tf_op jit(solution)/shard_map/reshape | solution.py:340
  (6 shorter events, 0.0 us)
Async XLA Ops:
  6.5 1.1 copy-start
  6.5 3.1 %copy-start.1 = (f32[48,40,40]{0,2,1:T(8,128)S(1)}, f32[48,40,40]{0,2,1:T(8,128)}, u32[]{:S(2)}) copy-start(f32[48,40,40]{0,2,1:T(8,128)} %param.7) | copy-start | bytes 921604
  6.5 75.6 %all-gather.2.cloned.1.call-start = ((), (), s32[]{:S(2)}) async-start(), calls=%async_computation | async-start | bytes 6758400 | tf_op jit(solution)/shard_map/all_gather | solution.py:278
  8.5 3.9 %copy-start.2 = (s32[1,2,32]{2,1,0:T(2,128)S(1)}, s32[1,2,32]{2,1,0:T(2,128)}, u32[]{:S(2)}) copy-start(s32[1,2,32]{2,1,0:T(2,128)} %param.5) | copy-start | bytes 772
  8.5 4.5 %copy-start.3 = (s32[1,2,32]{2,1,0:T(2,128)S(1)}, s32[1,2,32]{2,1,0:T(2,128)}, u32[]{:S(2)}) copy-start(s32[1,2,32]{2,1,0:T(2,128)} %param.6) | copy-start | bytes 772
Sparse Core Ops, SparseCore 0:
  10.2 71.8 all-gather.1

commit v2 on v1

--- a/solution.py
+++ b/solution.py
@@ -76,17 +76,31 @@
 
 
 def unfold_kernel(
-    held, per_tile, orbitals, scale, irr_ref, sym_ref, blocks_ref, right_ref, left_ref, out_ref, unfolded
+    held, per_tile, orbitals, scale, irr_ref, sym_ref, blocks_ref, rep_ref, turned_ref, out_ref, unfolded, right_ref, left_ref
 ):
     wide, steps, _, rows_y, _, _ = out_ref.shape
-    points = irr_ref.shape[0]
-    length = points // rows_y
+    length = irr_ref.shape[2]
+    points = rows_y * length
     lane = lax.broadcasted_iota(jnp.int32, (orbitals, LANES), 1)
     first = lane < orbitals
 
+    def one_table(sym, carry):
+        rep, turned = rep_ref[sym], turned_ref[sym]
+        high = rep.astype(jnp.bfloat16).astype(jnp.float32)
+        rest = jnp.zeros((orbitals, LANES - 3 * orbitals), jnp.float32)
+        left_ref[sym] = jnp.concatenate([high, high, rep - high, rest], axis=1)
+        before = (per_tile - 1) * orbitals
+        right_ref[sym, 0:before, :] = jnp.zeros((before, LANES), jnp.float32)
+        rest = jnp.zeros((orbitals, LANES - 2 * orbitals), jnp.float32)
+        right_ref[sym, before : before + orbitals, :] = jnp.concatenate([turned, turned, rest], axis=1)
+        right_ref[sym, before + orbitals :, :] = jnp.zeros((LANES - orbitals, LANES), jnp.float32)
+        return carry
+
+    lax.fori_loop(0, rep_ref.shape[0], one_table, 0, unroll=2)
+
     def one_point(k, carry):
-        irr = irr_ref[k]
-        sym = sym_ref[k]
+        irr = irr_ref[0, k // length, lax.rem(k, length)]
+        sym = sym_ref[0, k // length, lax.rem(k, length)]
         owner = irr // held
         row = irr - owner * held
         tile = row // per_tile
@@ -254,6 +268,103 @@
             narrow_copy(step, i).wait_send()
 
 
+def gather_kernel(own_ref, out_ref, send, recv, local_sem):
+    depth = out_ref.shape[0] // 2
+    wide, narrow = lax.axis_index("wide"), lax.axis_index("narrow")
+    z, x = wide // 2, lax.rem(wide, 2)
+    y, core = narrow // 2, lax.rem(narrow, 2)
+    other_x = z * 2 + 1 - x
+    other_y = (1 - y) * 2 + core
+    x_peer, y_peer = (other_x, narrow), (wide, other_y)
+    core_peer = (wide, y * 2 + 1 - core)
+    z_peers = [(lax.rem(z + i, depth) * 2 + x, narrow) for i in range(1, depth)]
+
+    barrier = pltpu.get_barrier_semaphore()
+    for peer in z_peers + [x_peer, y_peer, core_peer]:
+        pl.semaphore_signal(barrier, inc=1, device_id=peer, device_id_type=MESH)
+    pl.semaphore_wait(barrier, depth + 2)
+
+    mine = pltpu.make_async_copy(own_ref, out_ref.at[wide, narrow], local_sem)
+    mine.start()
+    copies = {}
+
+    def push(name, peer, block):
+        at = len(copies)
+        source = own_ref if block is None else out_ref.at[block]
+        target = (wide, narrow) if block is None else block
+        copies[name] = pltpu.make_async_remote_copy(
+            src_ref=source,
+            dst_ref=out_ref.at[target],
+            send_sem=send.at[at],
+            recv_sem=recv.at[at],
+            device_id=peer,
+            device_id_type=MESH,
+        )
+        copies[name].start()
+
+    def held(j, other_wide, other_narrow):
+        source = lax.rem(z + depth - j, depth) * 2 + (1 - x if other_wide else x)
+        return source, other_y if other_narrow else narrow
+
+    push("x0", x_peer, None)
+    push("y0", y_peer, None)
+    for i in range(1, depth):
+        push(f"z{i}", z_peers[i - 1], None)
+    push("c0", core_peer, None)
+
+    def arrived_z(j):
+        copies[f"z{j}"].wait_recv()
+        push(f"x{j}", x_peer, held(j, False, False))
+        push(f"y{j}", y_peer, held(j, False, False))
+        push(f"c{j}", core_peer, held(j, False, False))
+
+    def arrived_xy(j):
+        copies[f"x{j}"].wait_recv()
+        if 2 * j < depth:
+            push(f"yx{j}", y_peer, held(j, True, False))
+        push(f"cx{j}", core_peer, held(j, True, False))
+        copies[f"y{j}"].wait_recv()
+        if 2 * j >= depth:
+            push(f"xy{j}", x_peer, held(j, False, True))
+        push(f"cy{j}", core_peer, held(j, False, True))
+
+    for j in range(depth):
+        if j + 1 < depth:
+            arrived_z(j + 1)
+        arrived_xy(j)
+    for j in range(depth):
+        copies[f"yx{j}" if 2 * j < depth else f"xy{j}"].wait_recv()
+        push(f"cxy{j}", core_peer, held(j, True, True))
+    for name, copy in copies.items():
+        if name[0] == "c":
+            copy.wait_recv()
+    for copy in copies.values():
+        copy.wait_send()
+    mine.wait()
+
+
+def gather_blocks(own):
+    wide, narrow = lax.axis_size("wide"), lax.axis_size("narrow")
+    rows, columns = own.shape
+    count = wide * narrow - 1
+    vmem = pl.BlockSpec(memory_space=pltpu.VMEM)
+    every = pl.pallas_call(
+        gather_kernel,
+        out_shape=jax.ShapeDtypeStruct((wide, narrow, rows, columns), jnp.float32),
+        in_specs=[vmem],
+        out_specs=vmem,
+        scratch_shapes=[
+            pltpu.SemaphoreType.DMA((count,)),
+            pltpu.SemaphoreType.DMA((count,)),
+            pltpu.SemaphoreType.DMA,
+        ],
+        compiler_params=pltpu.CompilerParams(
+            collective_id=1, has_side_effects=True, vmem_limit_bytes=32 * 1024 * 1024
+        ),
+    )(own)
+    return every.reshape(wide, narrow * rows, columns)
+
+
 def spread_blocks(sigma_irr, orbitals, per_tile):
     held, freqs, parts, _ = sigma_irr.shape
     narrow = lax.axis_size("narrow")
@@ -275,6 +386,8 @@
     own = own.reshape(rows, tiles, per_tile * orbitals)
     own = jnp.pad(own, ((0, 0), (0, 0), (0, LANES - per_tile * orbitals)))
     own = own.reshape(rows, tiles * LANES)
+    if (lax.axis_size("wide"), narrow) == (8, 4) and len(axes) == 2:
+        return gather_blocks(own)
     every = lax.all_gather(own, axes, axis=0, tiled=True)
     return every.reshape(lax.axis_size("wide"), freqs * parts * orbitals, tiles * LANES)
 
@@ -282,7 +395,7 @@
 def local(sigma_irr, star_irr, star_sym, rep_matrices):
     wide, narrow = lax.axis_size("wide"), lax.axis_size("narrow")
     held, freqs, parts, _ = sigma_irr.shape
-    orbitals = rep_matrices.shape[1]
+    syms, orbitals = rep_matrices.shape[:2]
     rows_y, length = star_irr.shape[1:]
     per_tile = LANES // orbitals
     per_dest = length // wide
@@ -292,17 +405,6 @@
     rows_x = size_x // narrow
 
     blocks = spread_blocks(sigma_irr, orbitals, per_tile)
-    turned = jnp.swapaxes(rep_matrices, 1, 2)
-    before = (per_tile - 1) * orbitals
-    right = jnp.pad(
-        jnp.concatenate([turned, turned], axis=2),
-        ((0, 0), (before, LANES - orbitals), (0, LANES - 2 * orbitals)),
-    )
-    high = lax.reduce_precision(rep_matrices, 8, 7)
-    left = jnp.pad(
-        jnp.concatenate([high, high, rep_matrices - high], axis=2), ((0, 0), (0, 0), (0, LANES - 3 * orbitals))
-    )
-
     vmem = pl.BlockSpec(memory_space=pltpu.VMEM)
     smem = pl.BlockSpec(memory_space=pltpu.SMEM)
     sent = pl.pallas_call(
@@ -312,9 +414,13 @@
         out_shape=jax.ShapeDtypeStruct((wide, steps, 2, rows_y, tile_rows, LANES), jnp.float32),
         in_specs=[smem, smem, vmem, vmem, vmem],
         out_specs=vmem,
-        scratch_shapes=[pltpu.VMEM((2, rows_y * length, orbitals, LANES), jnp.float32)],
+        scratch_shapes=[
+            pltpu.VMEM((2, rows_y * length, orbitals, LANES), jnp.float32),
+            pltpu.VMEM((syms, per_tile * orbitals + LANES - orbitals, LANES), jnp.float32),
+            pltpu.VMEM((syms, orbitals, LANES), jnp.float32),
+        ],
         compiler_params=pltpu.CompilerParams(vmem_limit_bytes=56 * 1024 * 1024),
-    )(star_irr.reshape(-1), star_sym.reshape(-1), blocks, right, left)
+    )(star_irr, star_sym, blocks, rep_matrices, jnp.swapaxes(rep_matrices, 1, 2))
 
     slots = (steps, 2, rows_y, tile_rows, LANES)
     middle = (narrow, steps, rows_x, 2, rows_y, tile_rows, LANES)

time: 171 us -> 135 us (0.79)
  waiting for transfers between devices: 61.4 us -> 0 us
  Pallas kernels: 75.9 us -> 121 us
  between operations: 13.5 us -> 0.09 us
  other arithmetic: 6.6 us -> 0 us
    all_gather x1 -> x0, waiting for transfers between devices: 61.4 us -> none  [spread_blocks(): every = lax.all_gather(own, axes, axis=0, tiled=True)]
    pallas_call x0 -> x1, Pallas kernels: none -> 38.9 us  [gather_blocks(): pl.pallas_call(gather_kernel, out_shape=jax.ShapeDtypeStruct((wide, narro...]
    pallas_call x1, Pallas kernels: 56.2 us -> 61.4 us  [local(): pl.pallas_call(functools.partial(exchange_kernel, orbitals), out_shape=ja...]
    concatenate x2 -> x0, other arithmetic: 4.24 us -> none  [the longest x1 2.64 us: local(): jnp.concatenate([turned, turned], axis=2)]
    unnamed x12 -> x10, local copies, waits for them, and re-layouts: 3.7 us -> 6.72 us
  transfers between devices with their start and end apart: 1 -> 0, of which waited for: 1 -> 0; matrix products, arithmetic and copies ran while one was open for 7% -> 0% of each run, Pallas kernels for 0% -> 0%
where the time goes in v2:
time: 135 us
  Pallas kernels  121 us (90%)
  local copies, waits for them, and re-layouts  14 us (10%)
    pallas_call x1, Pallas kernels, local(): pl.pallas_call(functools.partial(exchange_kernel, orbitals), out_shape=ja...  61.4 us
    pallas_call x1, Pallas kernels, gather_blocks(): pl.pallas_call(gather_kernel, out_shape=jax.ShapeDtypeStruct((wide, narro...  38.9 us
    pallas_call x1, Pallas kernels, local(): pl.pallas_call(functools.partial(unfold_kernel, held, per_tile, orbitals,...  20.8 us
    unnamed x10, local copies, waits for them, and re-layouts  6.72 us
    reshape x1, local copies, waits for them, and re-layouts, local(): return result.reshape(result.shape[:5] + (orbitals * orbitals,))  6.22 us

profile of v2, /device:TPU:11, one launch (start us, length us, event | category | flops | bytes accessed | tf_op | source)
XLA Modules:
  0.0 135.1 jit_solution(5523873619989625846)
XLA Ops:
  0.0 0.0 copy-start
  0.0 0.0 copy-start.2
  0.0 1.1 copy-done
  1.1 0.5 dynamic-slice_reduce_fusion
  1.7 0.3 reshape.15
  1.9 0.1 copy.10
  2.0 0.1 pad.8.clone
  2.1 0.2 reshape.16
  2.3 0.1 copy.13
  2.4 0.0 copy-done.2
  2.4 1.3 copy.9.rep_ref
  3.7 1.4 %copy.8 = f32[48,40,40]{1,2,0:T(8,128)} copy(f32[48,40,40]{0,2,1:T(8,128)S(1)} %copy-done.2) | data formatting | bytes 614400 | tf_op args[3]
  5.1 38.9 %shard_map.46 = f32[8,4,40,1280]{3,2,1,0:T(8,128)S(1)} custom-call(f32[40,1280]{1,0:T(8,128)S(1)} %bitcast.10), custom_call_target="tpu_custom_call" | custom-call | tf_op jit(solution)/shard_map/pallas_call | solution.py:351
  43.9 0.0 copy-start.1
  43.9 2.7 %copy-done.1 = f32[8,4,40,1280]{3,2,1,0:T(8,128)} copy-done((f32[8,4,40,1280]{3,2,1,0:T(8,128)}, f32[8,4,40,1280]{3,2,1,0:T(8,128)S(1)}, u32[]{:S(2)}) %copy-start.1) | copy-done | bytes 6553624
  46.7 20.8 %shard_map.47.y_ref = f32[8,5,2,2,24,128]{5,4,3,2,1,0:T(8,128)} custom-call(s32[1,2,32]{2,1,0:T(2,128)} %irr_ref.1, s32[1,2,32]{2,1,0:T(2,128)} %sym_ref.1, f32[8,160,1280]{2,1,0:T(8,128)} %bitcast.9, f32[48,40,40]{2,1,0:T(8,128)} %copy.9.rep_ref, f32[48,40,40]{2,1,0:T(8,128)} %bitcast.11), custom_call_target="tpu_custom_call" | custom-call | tf_op jit(solution)/shard_map/pallas_call | solution.py:410
  67.5 61.4 %shard_map.48 = f32[2,8,4,2,2,40,40]{6,5,4,3,2,1,0:T(8,128)} custom-call(f32[8,5,2,2,24,128]{5,4,3,2,1,0:T(8,128)} %shard_map.47.y_ref), custom_call_target="tpu_custom_call" | custom-call | tf_op jit(solution)/shard_map/pallas_call | solution.py:427
  128.8 6.2 %reshape.19 = f32[2,8,4,2,2,1600]{5,4,3,2,1,0:T(2,128)} reshape(f32[2,8,4,2,2,40,40]{6,5,4,3,2,1,0:T(8,128)} %shard_map.48) | data formatting | bytes 3276800 | tf_op jit(solution)/shard_map/reshape | solution.py:446
  (1 shorter events, 0.0 us)
Async XLA Ops:
  0.0 1.1 copy-start
  0.0 2.4 %copy-start.2 = (f32[48,40,40]{0,2,1:T(8,128)S(1)}, f32[48,40,40]{0,2,1:T(8,128)}, u32[]{:S(2)}) copy-start(f32[48,40,40]{0,2,1:T(8,128)} %param.7) | copy-start | bytes 921604
  43.9 2.7 %copy-start.1 = (f32[8,4,40,1280]{3,2,1,0:T(8,128)}, f32[8,4,40,1280]{3,2,1,0:T(8,128)S(1)}, u32[]{:S(2)}) copy-start(f32[8,4,40,1280]{3,2,1,0:T(8,128)S(1)} %shard_map.46) | copy-start | bytes 19660804

commit v3 on v2

--- a/solution.py
+++ b/solution.py
@@ -78,8 +78,9 @@
 def unfold_kernel(
     held, per_tile, orbitals, scale, irr_ref, sym_ref, blocks_ref, rep_ref, turned_ref, out_ref, unfolded, right_ref, left_ref
 ):
-    wide, steps, _, rows_y, _, _ = out_ref.shape
-    length = irr_ref.shape[2]
+    wide, steps, _, _, _ = out_ref.shape
+    rows_y, length = irr_ref.shape[1:]
+    full = out_ref.shape[3] // SUB // rows_y
     points = rows_y * length
     lane = lax.broadcasted_iota(jnp.int32, (orbitals, LANES), 1)
     first = lane < orbitals
@@ -147,9 +148,7 @@
 
     per_dest = length // wide
 
-    def one_transform(at, carry):
-        y = at // steps
-        step = at - y * steps
+    def one_transform(y, step, carry):
         rows = pl.ds(pl.multiple_of(step * SUB, SUB), SUB)
         values = [(unfolded[0, y * length + z, rows, :], unfolded[1, y * length + z, rows, :]) for z in range(length)]
         result = fourier(values)
@@ -157,18 +156,27 @@
             for c in range(2):
                 made = pack([result[dest * per_dest + i][c] * scale for i in range(per_dest)], 2 * orbitals)
                 for j, tile in enumerate(made):
-                    out_ref[dest, step, c, y, j * SUB : (j + 1) * SUB, :] = tile
+                    at = (y * full + j if j < full else rows_y * full) * SUB
+                    if j == full and y:
+                        shared = out_ref[dest, step, c, at : at + SUB, :]
+                        where = lax.broadcasted_iota(jnp.int32, tile.shape, 1)
+                        tile = jnp.where(where < LANES // 2, shared, pltpu.roll(tile, LANES // 2, 1))
+                    out_ref[dest, step, c, at : at + SUB, :] = tile
         return carry
 
-    lax.fori_loop(0, rows_y * steps, one_transform, 0)
+    for y in range(rows_y):
+        lax.fori_loop(0, steps, functools.partial(one_transform, y), 0)
 
 
 def exchange_kernel(
     orbitals, y_ref, out_ref, from_wide, to_narrow, from_narrow, send_wide, recv_wide, send_narrow, recv_narrow, own
 ):
-    wide, steps, _, rows_y, tile_rows, _ = y_ref.shape
+    wide, steps, _, tile_rows, _ = y_ref.shape
     narrow, _, rows_x = to_narrow.shape[:3]
+    rows_y = out_ref.shape[1] // narrow
     tiles = tile_rows // SUB
+    full = tiles // rows_y
+    lines = full + tiles % rows_y
     me_wide = lax.axis_index("wide")
     me_narrow = lax.axis_index("narrow")
 
@@ -215,20 +223,19 @@
 
         def one(x, carry):
             made = []
-            for j in range(tiles):
-                at = slice(j * SUB, (j + 1) * SUB)
-                made.append(
-                    fourier(
-                        [
-                            (from_narrow[n, step, x, 0, y, at, :], from_narrow[n, step, x, 1, y, at, :])
-                            for n in range(narrow)
-                            for y in range(rows_y)
-                        ]
-                    )
-                )
+            for j in range(lines):
+                values = []
+                for n in range(narrow):
+                    for y in range(rows_y):
+                        at = (y * full + j if j < full else rows_y * full) * SUB
+                        pair = [from_narrow[n, step, x, c, at : at + SUB, :] for c in range(2)]
+                        if j == full and y:
+                            pair = [pltpu.roll(value, LANES // 2, 1) for value in pair]
+                        values.append(tuple(pair))
+                made.append(fourier(values))
             for y in range(narrow * rows_y):
                 for c in range(2):
-                    line = [made[j][y][c] for j in range(tiles)]
+                    line = [made[j][y][c] for j in range(lines)]
                     for z in range(out_ref.shape[2]):
                         for f in range(2):
                             block = unpack(line, 2 * z + f, orbitals)
@@ -242,17 +249,14 @@
             wide_copy(step, i).wait_recv()
 
         def one(at, carry):
-            y = at // tiles
-            rows = pl.ds(pl.multiple_of((at - y * tiles) * SUB, SUB), SUB)
-            values = [
-                (from_wide[w, step, 0, y, rows, :], from_wide[w, step, 1, y, rows, :]) for w in range(wide)
-            ]
+            rows = pl.ds(pl.multiple_of(at * SUB, SUB), SUB)
+            values = [(from_wide[w, step, 0, rows, :], from_wide[w, step, 1, rows, :]) for w in range(wide)]
             for x, pair in enumerate(fourier(values)):
                 for c in range(2):
-                    to_narrow[x // rows_x, step, x % rows_x, c, y, rows, :] = pair[c]
+                    to_narrow[x // rows_x, step, x % rows_x, c, rows, :] = pair[c]
             return carry
 
-        lax.fori_loop(0, rows_y * tiles, one, 0)
+        lax.fori_loop(0, tiles, one, 0)
         for i in range(1, narrow):
             narrow_copy(step, i).start()
         mine = pltpu.make_async_copy(to_narrow.at[me_narrow, step], from_narrow.at[me_narrow, step], own.at[step])
@@ -400,7 +404,11 @@
     per_tile = LANES // orbitals
     per_dest = length // wide
     steps = orbitals // SUB
-    tile_rows = SUB * -(-per_dest * freqs * orbitals // LANES)
+    used = per_dest * freqs * orbitals
+    if rows_y == 2 and used % LANES == LANES // 2:
+        tile_rows = SUB * (2 * used // LANES)
+    else:
+        tile_rows = SUB * rows_y * -(-used // LANES)
     size_x, size_y = wide * star_irr.shape[0], narrow * rows_y
     rows_x = size_x // narrow
 
@@ -411,7 +419,7 @@
         functools.partial(
             unfold_kernel, held, per_tile, orbitals, 1.0 / math.sqrt(size_x * size_y * length)
         ),
-        out_shape=jax.ShapeDtypeStruct((wide, steps, 2, rows_y, tile_rows, LANES), jnp.float32),
+        out_shape=jax.ShapeDtypeStruct((wide, steps, 2, tile_rows, LANES), jnp.float32),
         in_specs=[smem, smem, vmem, vmem, vmem],
         out_specs=vmem,
         scratch_shapes=[
@@ -422,8 +430,8 @@
         compiler_params=pltpu.CompilerParams(vmem_limit_bytes=56 * 1024 * 1024),
     )(star_irr, star_sym, blocks, rep_matrices, jnp.swapaxes(rep_matrices, 1, 2))
 
-    slots = (steps, 2, rows_y, tile_rows, LANES)
-    middle = (narrow, steps, rows_x, 2, rows_y, tile_rows, LANES)
+    slots = (steps, 2, tile_rows, LANES)
+    middle = (narrow, steps, rows_x, 2, tile_rows, LANES)
     result = pl.pallas_call(
         functools.partial(exchange_kernel, orbitals),
         out_shape=jax.ShapeDtypeStruct((rows_x, size_y, per_dest, freqs, 2, orbitals, orbitals), jnp.float32),

time: 135 us -> 128 us (0.948)
  Pallas kernels: 121 us -> 113 us
    pallas_call x1, Pallas kernels: 61.4 us -> 53.5 us  [local(): pl.pallas_call(functools.partial(exchange_kernel, orbitals), out_shape=ja...]
where the time goes in v3:
time: 128 us; the launch traced here: 127 us
  Pallas kernels  113 us (88%)
  local copies, waits for them, and re-layouts  14 us (11%)
    pallas_call x1, Pallas kernels, local(): pl.pallas_call(functools.partial(exchange_kernel, orbitals), out_shape=ja...  53.5 us
    pallas_call x1, Pallas kernels, gather_blocks(): pl.pallas_call(gather_kernel, out_shape=jax.ShapeDtypeStruct((wide, narro...  38.9 us
    pallas_call x1, Pallas kernels, local(): pl.pallas_call(functools.partial(unfold_kernel, held, per_tile, orbitals,...  20.8 us
    unnamed x10, local copies, waits for them, and re-layouts  6.71 us
    reshape x1, local copies, waits for them, and re-layouts, local(): return result.reshape(result.shape[:5] + (orbitals * orbitals,))  6.22 us

profile of v3, /device:TPU:11, one launch (start us, length us, event | category | flops | bytes accessed | tf_op | source)
XLA Modules:
  0.0 127.2 jit_solution(6072705480096534567)
XLA Ops:
  0.0 0.0 copy-start
  0.0 0.0 copy-start.2
  0.0 1.1 copy-done
  1.1 0.5 dynamic-slice_reduce_fusion
  1.7 0.3 reshape.15
  1.9 0.1 copy.10
  2.0 0.1 pad.8.clone
  2.1 0.2 reshape.16
  2.3 0.1 copy.13
  2.4 0.0 copy-done.2
  2.4 1.3 %copy.9.rep_ref = f32[48,40,40]{2,1,0:T(8,128)} copy(f32[48,40,40]{0,2,1:T(8,128)S(1)} %copy-done.2) | data formatting | bytes 614400 | tf_op args[3]
  3.7 1.4 %copy.8 = f32[48,40,40]{1,2,0:T(8,128)} copy(f32[48,40,40]{0,2,1:T(8,128)S(1)} %copy-done.2) | data formatting | bytes 614400 | tf_op args[3]
  5.1 38.9 %shard_map.46 = f32[8,4,40,1280]{3,2,1,0:T(8,128)S(1)} custom-call(f32[40,1280]{1,0:T(8,128)S(1)} %bitcast.10), custom_call_target="tpu_custom_call" | custom-call | tf_op jit(solution)/shard_map/pallas_call | solution.py:355
  43.9 0.0 copy-start.1
  43.9 2.7 %copy-done.1 = f32[8,4,40,1280]{3,2,1,0:T(8,128)} copy-done((f32[8,4,40,1280]{3,2,1,0:T(8,128)}, f32[8,4,40,1280]{3,2,1,0:T(8,128)S(1)}, u32[]{:S(2)}) %copy-start.1) | copy-done | bytes 6553624
  46.7 20.8 %shard_map.47.y_ref = f32[8,5,2,40,128]{4,3,2,1,0:T(8,128)} custom-call(s32[1,2,32]{2,1,0:T(2,128)} %irr_ref.1, s32[1,2,32]{2,1,0:T(2,128)} %sym_ref.1, f32[8,160,1280]{2,1,0:T(8,128)} %bitcast.9, f32[48,40,40]{2,1,0:T(8,128)} %copy.9.rep_ref, f32[48,40,40]{2,1,0:T(8,128)} %bitcast.11), custom_call_target="tpu_custom_call" | custom-call | tf_op jit(solution)/shard_map/pallas_call | solution.py:418
  67.5 53.5 %shard_map.48 = f32[2,8,4,2,2,40,40]{6,5,4,3,2,1,0:T(8,128)} custom-call(f32[8,5,2,40,128]{4,3,2,1,0:T(8,128)} %shard_map.47.y_ref), custom_call_target="tpu_custom_call" | custom-call | tf_op jit(solution)/shard_map/pallas_call | solution.py:435
  120.9 6.2 %reshape.19 = f32[2,8,4,2,2,1600]{5,4,3,2,1,0:T(2,128)} reshape(f32[2,8,4,2,2,40,40]{6,5,4,3,2,1,0:T(8,128)} %shard_map.48) | data formatting | bytes 3276800 | tf_op jit(solution)/shard_map/reshape | solution.py:454
  (1 shorter events, 0.0 us)
Async XLA Ops:
  0.0 1.1 copy-start
  0.0 2.4 %copy-start.2 = (f32[48,40,40]{0,2,1:T(8,128)S(1)}, f32[48,40,40]{0,2,1:T(8,128)}, u32[]{:S(2)}) copy-start(f32[48,40,40]{0,2,1:T(8,128)} %param.7) | copy-start | bytes 921604
  43.9 2.7 %copy-start.1 = (f32[8,4,40,1280]{3,2,1,0:T(8,128)}, f32[8,4,40,1280]{3,2,1,0:T(8,128)S(1)}, u32[]{:S(2)}) copy-start(f32[8,4,40,1280]{3,2,1,0:T(8,128)S(1)} %shard_map.46) | copy-start | bytes 19660804

commit v4 on v3

--- a/solution.py
+++ b/solution.py
@@ -144,7 +144,7 @@
         unfolded[1, k] = turned[:, LANES:]
         return carry
 
-    lax.fori_loop(0, points, one_point, 0, unroll=4)
+    lax.fori_loop(0, points, one_point, 0, unroll=8)
 
     per_dest = length // wide
 
@@ -356,7 +356,7 @@
         gather_kernel,
         out_shape=jax.ShapeDtypeStruct((wide, narrow, rows, columns), jnp.float32),
         in_specs=[vmem],
-        out_specs=vmem,
+        out_specs=pl.BlockSpec(memory_space=pl.ANY),
         scratch_shapes=[
             pltpu.SemaphoreType.DMA((count,)),
             pltpu.SemaphoreType.DMA((count,)),

time: 128 us -> 125 us (0.977)
  Pallas kernels: 113 us -> 111 us
    pallas_call x1, Pallas kernels: 20.8 us -> 18.7 us  [local(): pl.pallas_call(functools.partial(unfold_kernel, held, per_tile, orbitals,...]
where the time goes in v4:
time: 125 us
  Pallas kernels  111 us (89%)
  local copies, waits for them, and re-layouts  14 us (11%)
    pallas_call x1, Pallas kernels, local(): pl.pallas_call(functools.partial(exchange_kernel, orbitals), out_shape=ja...  53.5 us
    pallas_call x1, Pallas kernels, gather_blocks(): pl.pallas_call(gather_kernel, out_shape=jax.ShapeDtypeStruct((wide, narro...  38.9 us
    pallas_call x1, Pallas kernels, local(): pl.pallas_call(functools.partial(unfold_kernel, held, per_tile, orbitals,...  18.7 us
    unnamed x10, local copies, waits for them, and re-layouts  6.71 us
    reshape x1, local copies, waits for them, and re-layouts, local(): return result.reshape(result.shape[:5] + (orbitals * orbitals,))  6.22 us

profile of v4, /device:TPU:11, one launch (start us, length us, event | category | flops | bytes accessed | tf_op | source)
XLA Modules:
  0.0 125.1 jit_solution(6189124522845352456)
XLA Ops:
  0.0 0.0 copy-start
  0.0 0.0 copy-start.2
  0.0 1.1 copy-done
  1.1 0.5 dynamic-slice_reduce_fusion
  1.7 0.3 reshape.15
  1.9 0.1 copy.10
  2.0 0.1 pad.8.clone
  2.1 0.2 reshape.16
  2.3 0.1 copy.13
  2.4 0.0 copy-done.2
  2.4 1.3 %copy.9.rep_ref = f32[48,40,40]{2,1,0:T(8,128)} copy(f32[48,40,40]{0,2,1:T(8,128)S(1)} %copy-done.2) | data formatting | bytes 614400 | tf_op args[3]
  3.7 1.4 %copy.8 = f32[48,40,40]{1,2,0:T(8,128)} copy(f32[48,40,40]{0,2,1:T(8,128)S(1)} %copy-done.2) | data formatting | bytes 614400 | tf_op args[3]
  5.1 38.9 %shard_map.46 = f32[8,4,40,1280]{3,2,1,0:T(8,128)S(1)} custom-call(f32[40,1280]{1,0:T(8,128)S(1)} %bitcast.10), custom_call_target="tpu_custom_call" | custom-call | tf_op jit(solution)/shard_map/pallas_call | solution.py:355
  43.9 0.0 copy-start.1
  43.9 2.7 %copy-done.1 = f32[8,4,40,1280]{3,2,1,0:T(8,128)} copy-done((f32[8,4,40,1280]{3,2,1,0:T(8,128)}, f32[8,4,40,1280]{3,2,1,0:T(8,128)S(1)}, u32[]{:S(2)}) %copy-start.1) | copy-done | bytes 6553624
  46.7 18.7 %shard_map.47.y_ref = f32[8,5,2,40,128]{4,3,2,1,0:T(8,128)} custom-call(s32[1,2,32]{2,1,0:T(2,128)} %irr_ref.1, s32[1,2,32]{2,1,0:T(2,128)} %sym_ref.1, f32[8,160,1280]{2,1,0:T(8,128)} %bitcast.9, f32[48,40,40]{2,1,0:T(8,128)} %copy.9.rep_ref, f32[48,40,40]{2,1,0:T(8,128)} %bitcast.11), custom_call_target="tpu_custom_call" | custom-call | tf_op jit(solution)/shard_map/pallas_call | solution.py:418
  65.4 53.5 %shard_map.48 = f32[2,8,4,2,2,40,40]{6,5,4,3,2,1,0:T(8,128)} custom-call(f32[8,5,2,40,128]{4,3,2,1,0:T(8,128)} %shard_map.47.y_ref), custom_call_target="tpu_custom_call" | custom-call | tf_op jit(solution)/shard_map/pallas_call | solution.py:435
  118.9 6.2 %reshape.19 = f32[2,8,4,2,2,1600]{5,4,3,2,1,0:T(2,128)} reshape(f32[2,8,4,2,2,40,40]{6,5,4,3,2,1,0:T(8,128)} %shard_map.48) | data formatting | bytes 3276800 | tf_op jit(solution)/shard_map/reshape | solution.py:454
  (1 shorter events, 0.0 us)
Async XLA Ops:
  0.0 1.1 copy-start
  0.0 2.4 %copy-start.2 = (f32[48,40,40]{0,2,1:T(8,128)S(1)}, f32[48,40,40]{0,2,1:T(8,128)}, u32[]{:S(2)}) copy-start(f32[48,40,40]{0,2,1:T(8,128)} %param.7) | copy-start | bytes 921604
  43.9 2.7 %copy-start.1 = (f32[8,4,40,1280]{3,2,1,0:T(8,128)}, f32[8,4,40,1280]{3,2,1,0:T(8,128)S(1)}, u32[]{:S(2)}) copy-start(f32[8,4,40,1280]{3,2,1,0:T(8,128)S(1)} %shard_map.46) | copy-start | bytes 19660804
